TPU v7x, 32 devices: a whole 2x2x4 slice. The times are simulated.
32 devices in a mesh: rows: 4 (over y, core), cols: 8 (over z, x).
Axes of the slice: x: 2, y: 2, z: 4, core: 2. Of those that a mesh axis runs over, the one named last changes fastest.
Arguments:
- lot_features: bfloat16 [8192, 512], P(('rows', 'cols')), may hold values from -60 to 60
- slot_features: bfloat16 [8192, 512], P(('cols', 'rows')), may hold values from -60 to 60
- lot_mass: float32 [8192], P('rows'), may hold values from 0.5 to 2
- slot_mass: float32 [8192], P('cols'), may hold values from 0.5 to 2
Outputs:
- lot_grad: float32 [8192, 512], P(('rows', 'cols'))
All inputs are finite; a program needn't handle non-finite values.
Results may differ from a plain program's by a relative error of at most 0.0034.
Values may be sent and summed in bfloat16 or wider, within the bound.
A program may use at most 64 MiB of HBM per device.

v0:
```python
import jax
import jax.numpy as jnp
from jax import lax
from jax.sharding import PartitionSpec as P

ITERS = 3


EPS = 1.0


def combined_all(value, axis, join):
    pieces = jax.tree.map(lambda part: lax.all_gather(part, axis), value)
    head = jax.tree.map(lambda part: part[0], pieces)
    tail = jax.tree.map(lambda part: part[1:], pieces)
    total, _ = lax.scan(lambda total, share: (join(total, share), None), head, tail)
    return total


def combine(first, second):
    top = jnp.maximum(first[0], second[0])
    return (top, first[1] * jnp.exp(first[0] - top) + second[1] * jnp.exp(second[0] - top))


def local(lot_features, slot_features, lot_mass, slot_mass):
    lot_full = lax.all_gather(lot_features, "cols", axis=0, tiled=True)
    slot_full = lax.all_gather(slot_features, "rows", axis=0, tiled=True)
    width = lot_full.shape[1]
    lot_sq = jnp.sum(lot_full.astype(jnp.float32) ** 2, axis=1)
    slot_sq = jnp.sum(slot_full.astype(jnp.float32) ** 2, axis=1)
    cost_scale = 0.5 / width**0.5

    def make_tile():
        inner = lax.dot_general(
            lot_full, slot_full, (((1,), (1,)), ((), ())), preferred_element_type=jnp.float32
        )
        return (lot_sq[:, None] + slot_sq[None, :] - 2.0 * inner) * cost_scale

    def get_tile():
        return make_tile()

    log_lot = jnp.log(lot_mass)
    log_slot = jnp.log(slot_mass)
    slot_pot = jnp.zeros(slot_mass.shape, jnp.float32)
    lot_pot = jnp.zeros(lot_mass.shape, jnp.float32)
    for step in range(ITERS):
        scores = (slot_pot[None, :] - get_tile()) / EPS
        peaks = jnp.max(scores, axis=1)
        totals = jnp.sum(jnp.exp(scores - peaks[:, None]), axis=1)
        peaks, totals = combined_all((peaks, totals), "cols", combine)
        lot_pot = EPS * log_lot - EPS * (peaks + jnp.log(totals))
        scores = (lot_pot[:, None] - get_tile()) / EPS
        peaks = jnp.max(scores, axis=0)
        totals = jnp.sum(jnp.exp(scores - peaks[None, :]), axis=0)
        peaks, totals = combined_all((peaks, totals), "rows", combine)
        slot_pot = EPS * log_slot - EPS * (peaks + jnp.log(totals))
    plan = jnp.exp((lot_pot[:, None] + slot_pot[None, :] - get_tile()) / EPS)
    row_total = jnp.sum(plan, axis=1)
    moved = jnp.dot(plan.astype(jnp.bfloat16), slot_full, preferred_element_type=jnp.float32)
    own_rows = lot_features.shape[0]
    own_start = lax.axis_index("cols") * own_rows
    moved_sum, row_sum = lax.psum((moved, row_total), "cols")
    gradient = row_sum[:, None] * lot_full.astype(jnp.float32) - moved_sum
    return lax.dynamic_slice_in_dim(gradient, own_start, own_rows, 0)


def solution(mesh):
    placed = (P(("rows", "cols"), None), P(("cols", "rows"), None), P("rows"), P("cols"))
    return jax.shard_map(
        local, mesh=mesh, in_specs=placed, out_specs=P(("rows", "cols"), None), check_vma=False
    )
```

profile of v0, /device:TPU:0, one launch (start us, length us, event | category | flops | bytes accessed | tf_op | source)
XLA Modules:
  0.0 520.5 jit_solution(15875760895717036803)
XLA Ops:
  8.1 20.3 %all-gather.17.cloned.1.call-done = bf16[1024,512]{1,0:T(8,128)(2,1)} async-done(((bf16[256,512]{1,0:T(8,128)(2,1)}), bf16[1024,512]{1,0:T(8,128)(2,1)}) %all-gather.17.cloned.1.call-update) | async-done | bytes 1048592 | tf_op jit(solution)/shard_map/all_gather | solution.py:27
  29.9 49.9 %all-gather.15.cloned.1.call-done = bf16[2048,512]{1,0:T(8,128)(2,1)} async-done(((bf16[256,512]{1,0:T(8,128)(2,1)}), bf16[2048,512]{1,0:T(8,128)(2,1)}) %all-gather.15.cloned.1.call-update) | async-done | bytes 2097168 | tf_op jit(solution)/shard_map/all_gather | solution.py:26
  81.9 4.4 subtract_reduce_fusion.5
  90.9 30.5 %all-gather.1 = f32[16384]{0:T(1024)S(1)} all-gather(f32[2048]{0:T(1024)S(1)} %exponential_reduce_fusion.5), channel_id=3, replica_groups=mesh['rows'=4,'cols'=8] {'cols'}, dimensions={0}, use_global_device_ids=true | all-gather | bytes 73728 | tf_op jit(solution)/shard_map/all_gather | solution.py:13
  121.4 30.5 %all-gather = f32[16384]{0:T(1024)S(1)} all-gather(f32[2048]{0:T(1024)S(1)} %get-tuple-element.269), channel_id=2, replica_groups=mesh['rows'=4,'cols'=8] {'cols'}, dimensions={0}, use_global_device_ids=true | all-gather | bytes 73728 | tf_op jit(solution)/shard_map/all_gather | solution.py:13
  152.5 4.2 subtract_reduce_fusion.4
  160.1 5.2 all-gather.2
  165.3 5.2 all-gather.3
  174.7 4.3 exponential_reduce_fusion.3
  179.0 30.5 %all-gather.4 = f32[16384]{0:T(1024)S(1)} all-gather(f32[2048]{0:T(1024)S(1)} %subtract_reduce_fusion.3), channel_id=6, replica_groups=mesh['rows'=4,'cols'=8] {'cols'}, dimensions={0}, use_global_device_ids=true | all-gather | bytes 73728 | tf_op jit(solution)/shard_map/all_gather | solution.py:13
  209.5 30.5 %all-gather.5 = f32[16384]{0:T(1024)S(1)} all-gather(f32[2048]{0:T(1024)S(1)} %exponential_reduce_fusion.3), channel_id=7, replica_groups=mesh['rows'=4,'cols'=8] {'cols'}, dimensions={0}, use_global_device_ids=true | all-gather | bytes 73728 | tf_op jit(solution)/shard_map/all_gather | solution.py:13
  244.6 4.4 exponential_reduce_fusion.2
  248.9 5.2 all-gather.6
  254.1 5.3 %all-gather.7 = f32[4096]{0:T(1024)S(1)} all-gather(f32[1024]{0:T(1024)S(1)} %exponential_reduce_fusion.2), channel_id=9, replica_groups=mesh['rows'=4,'cols'=8] {'rows'}, dimensions={0}, use_global_device_ids=true | all-gather | bytes 20480 | tf_op jit(solution)/shard_map/all_gather | solution.py:13
  263.7 4.3 exponential_reduce_fusion.1
  268.0 30.5 %all-gather.8 = f32[16384]{0:T(1024)S(1)} all-gather(f32[2048]{0:T(1024)S(1)} %subtract_reduce_fusion.1), channel_id=10, replica_groups=mesh['rows'=4,'cols'=8] {'cols'}, dimensions={0}, use_global_device_ids=true | all-gather | bytes 73728 | tf_op jit(solution)/shard_map/all_gather | solution.py:13
  298.5 30.5 %all-gather.9 = f32[16384]{0:T(1024)S(1)} all-gather(f32[2048]{0:T(1024)S(1)} %exponential_reduce_fusion.1), channel_id=11, replica_groups=mesh['rows'=4,'cols'=8] {'cols'}, dimensions={0}, use_global_device_ids=true | all-gather | bytes 73728 | tf_op jit(solution)/shard_map/all_gather | solution.py:13
  333.6 4.4 exponential_reduce_fusion
  338.0 5.2 all-gather.10
  343.2 5.2 all-gather.11
  348.6 7.9 %fusion.2 = f32[2048,512]{1,0:T(8,128)} fusion(bf16[1024,512]{1,0:T(8,128)(2,1)S(1)} %copy-done.3, f32[2048,1024]{0,1:T(8,128)} %copy-done, f32[1024]{0:T(1024)S(1)} %add_subtract_fusion.3, f32[2048]{0:T(1024)S(1)} %add_subtract_fusion), kind=kOutput, calls=%fused_computation.34 | convolution fusion | flops 2153775104 | bytes 13643776 | tf_op jit(solution)/shard_map/dot_general | solution.py:59
  356.5 4.4 fusion.1
  360.9 20.0 %psum.14 = f32[2048]{0:T(1024)S(1)} all-reduce(f32[2048]{0:T(1024)S(1)} %fusion.1), channel_id=1, replica_groups=mesh['rows'=4,'cols'=8] {'cols'}, use_global_device_ids=true, to_apply=%region_27.28 | all-reduce | flops 2048 | bytes 16384 | tf_op jit(solution)/shard_map/psum | solution.py:62
  383.5 128.4 %all-reduce.2.cloned.1.call-done = f32[2048,512]{1,0:T(8,128)} async-done(((f32[2048,512]{1,0:T(8,128)}), f32[2048,512]{1,0:T(8,128)}) %all-reduce.2.cloned.1.call-update) | async-done | bytes 4194320 | tf_op jit(solution)/shard_map/psum | solution.py:62
  (137 shorter events, 36.9 us)
Async XLA Ops:
  6.5 21.8 %all-gather.17.cloned.1.call-start = ((), (), s32[]{:S(2)}) async-start(), calls=%async_computation.1 | async-start | bytes 1310720 | tf_op jit(solution)/shard_map/all_gather | solution.py:27
  7.3 72.6 %all-gather.15.cloned.1.call-start = ((), (), s32[]{:S(2)}) async-start(), calls=%async_computation | async-start | bytes 2359296 | tf_op jit(solution)/shard_map/all_gather | solution.py:26
  8.0 503.9 %all-reduce.2.cloned.1.call-start = ((), (), s32[]{:S(2)}) async-start(), calls=%async_computation.2 | async-start | bytes 8388608 | tf_op jit(solution)/shard_map/psum | solution.py:62
  86.3 3.2 copy-start
  86.3 66.1 %copy-start.4 = (f32[2048]{0:T(1024)S(1)}, f32[2048]{0:T(1024)}, u32[]{:S(2)}) copy-start(f32[2048]{0:T(1024)} %param.18) | copy-start | bytes 24580
  152.4 5.8 %copy-start.1 = (f32[2048,1024]{0,1:T(8,128)S(1)}, f32[2048,1024]{0,1:T(8,128)}, u32[]{:S(2)}) copy-start(f32[2048,1024]{0,1:T(8,128)} %copy-done) | copy-start | bytes 25165828
  152.5 18.2 %copy-start.5 = (f32[1024]{0:T(1024)S(1)}, f32[1024]{0:T(1024)}, u32[]{:S(2)}) copy-start(f32[1024]{0:T(1024)} %param.19) | copy-start | bytes 12292
  329.5 19.0 %copy-start.3 = (bf16[1024,512]{1,0:T(8,128)(2,1)S(1)}, bf16[1024,512]{1,0:T(8,128)(2,1)}, u32[]{:S(2)}) copy-start(bf16[1024,512]{1,0:T(8,128)(2,1)} %all-gather.17.cloned.1.call-done) | copy-start | bytes 3145732
  356.5 24.5 %copy-start.2 = (bf16[2048,512]{1,0:T(8,128)(2,1)S(1)}, bf16[2048,512]{1,0:T(8,128)(2,1)}, u32[]{:S(2)}) copy-start(bf16[2048,512]{1,0:T(8,128)(2,1)} %all-gather.15.cloned.1.call-done) | copy-start | bytes 6291460
Sparse Core Ops, SparseCore 0:
  8.9 19.4 all-gather.16
  30.5 49.2 all-gather.14
  356.6 155.2 all-reduce.1
where the time goes:
time: 521 us
  blocking collectives  234 us (45%)
  waiting for transfers between devices  200 us (38%)
  other arithmetic  54 us (10%)
  between operations  13.5 us (3%)
  matrix products  12.3 us (2%)
  local copies, waits for them, and re-layouts  5.56 us (1%)
    all_gather x12, blocking collectives, combined_all(): pieces = jax.tree.map(lambda part: lax.all_gather(part, axis), value)  214 us
    psum x1, waiting for transfers between devices, local(): moved_sum, row_sum = lax.psum((moved, row_total), 'cols')  128 us
    all_gather x1, waiting for transfers between devices, local(): lot_full = lax.all_gather(lot_features, 'cols', axis=0, tiled=True)  49.9 us
    all_gather x1, waiting for transfers between devices, local(): slot_full = lax.all_gather(slot_features, 'rows', axis=0, tiled=True)  20.3 us
    psum x1, blocking collectives, local(): moved_sum, row_sum = lax.psum((moved, row_total), 'cols')  20 us
    reduce_max x3, other arithmetic, local(): peaks = jnp.max(scores, axis=0)  12.2 us
    reduce_sum x3, other arithmetic, local(): totals = jnp.sum(jnp.exp(scores - peaks[None, :]), axis=0)  10.7 us
  transfers between devices with their start and end apart: 3, of which 3 were waited for; matrix products, arithmetic and copies ran while one was open for 2% of the time, Pallas kernels for 0%

commit v1 on v0

v1 whole, which is shorter than its diff:
```python
import functools
import math

import jax
import jax.numpy as jnp
from jax import lax
from jax.experimental import pallas as pl
from jax.experimental.pallas import tpu as pltpu
from jax.sharding import PartitionSpec as P

ITERS = 3
LANES = 128
LOG2E = 1.0 / math.log(2.0)
MESH = pl.DeviceIdType.MESH


def near_first(size):
    table = []
    for here in range(size):
        others = sorted((abs(there - here), there) for there in range(size) if there != here)
        table.append([here] + [there for _, there in others])
    return table


def pick(table, here, step):
    value = jnp.int32(table[0][step])
    for index in range(1, len(table)):
        value = jnp.where(here == index, jnp.int32(table[index][step]), value)
    return value


def lse_rows(parts):
    top = functools.reduce(jnp.maximum, parts)
    total = functools.reduce(jnp.add, [jnp.exp2(part - top) for part in parts])
    return top + jnp.log2(total)


def kernel(
    n_rows, n_cols, x_ref, y_ref, lmass_ref, smass_ref, out_ref,
    x_all, y_all, tile, x_aux, y_aux, f_col, g_dense, mf, mg,
    row_parts, col_parts, plan, row_sum, sib_out, sib_in, far_out, far_in, acc,
    xh_send, xh_recv, xl_send, xl_recv, yh_send, yh_recv, yl_send, yl_recv,
    xa_send, xa_recv, ya_send, ya_recv, row_send, row_recv, col_send, col_recv,
    sib_send, sib_recv, far_send, far_recv,
):
    r = lax.axis_index("rows")
    c = lax.axis_index("cols")
    block, width = x_ref.shape
    per = block // LANES
    lots, slots = n_rows * block, n_cols * block
    lot_groups, slot_groups = lots // LANES, slots // LANES
    unit = LOG2E / width**0.5

    barrier = pltpu.get_barrier_semaphore()
    for d in range(1, n_rows):
        pl.semaphore_signal(barrier, inc=1, device_id=(lax.rem(r + d, n_rows), c), device_id_type=MESH)
    for d in range(1, n_cols):
        pl.semaphore_signal(barrier, inc=1, device_id=(r, lax.rem(c + d, n_cols)), device_id_type=MESH)
    pl.semaphore_wait(barrier, n_rows + n_cols - 2)

    pending = []

    def push(src, dst, send, recv, target, when=None):
        copy = pltpu.make_async_remote_copy(
            src_ref=src, dst_ref=dst, send_sem=send, recv_sem=recv,
            device_id=target, device_id_type=MESH,
        )
        if when is None:
            copy.start()
        else:
            pl.when(when)(copy.start)
        pending.append((copy, when))
        return copy

    def landed(dst, send, recv):
        pltpu.make_async_remote_copy(
            src_ref=dst, dst_ref=dst, send_sem=send, recv_sem=recv,
            device_id=(r, c), device_id_type=MESH,
        ).wait_recv()

    class Gather:
        def __init__(self, buf, own, hi, lo, index, target, h_send, h_recv, l_send, l_recv):
            self.buf, self.own, self.hi, self.lo = buf, own, hi, lo
            self.h, self.l = index // lo, lax.rem(index, lo)
            self.target = target
            self.sems = h_send, h_recv, l_send, l_recv
            self.table = near_first(hi)

        def place(self, h, l):
            return pl.ds(pl.multiple_of((h * self.lo + l) * block, block), block)

        def step(self, j):
            h_send, h_recv, l_send, l_recv = self.sems
            src_h = self.h if j == 0 else pick(self.table, self.h, j)
            dst = self.buf.at[self.place(src_h, self.l)]
            if j == 0:
                src = self.own
                for way in (0, 1):
                    to = self.h + (2 * way - 1)
                    ok = jnp.logical_and(to >= 0, to < self.hi)
                    push(src, dst, h_send.at[way, 0], h_recv.at[src_h], self.target(to, self.l), ok)
            else:
                src = dst
                landed(dst, h_send.at[0, j], h_recv.at[src_h])
                to = jnp.where(src_h < self.h, self.h + 1, self.h - 1)
                ok = jnp.logical_and(to >= 0, to < self.hi)
                push(src, dst, h_send.at[0, j], h_recv.at[src_h], self.target(to, self.l), ok)
            for e in range(1, self.lo):
                to = lax.rem(self.l + e, self.lo)
                push(src, dst, l_send.at[e, j], l_recv.at[self.l, src_h], self.target(self.h, to))
            return src_h * self.lo + self.l

        def cross(self, j, e):
            _, _, l_send, l_recv = self.sems
            src_h = self.h if j == 0 else pick(self.table, self.h, j)
            src_l = lax.rem(self.l + e, self.lo)
            landed(self.buf.at[self.place(src_h, src_l)], l_send.at[e, j], l_recv.at[src_l, src_h])
            return src_h * self.lo + src_l

    r_lo = 2 if n_rows % 2 == 0 else 1
    r_hi = n_rows // r_lo
    c_hi = 4 if n_cols % 4 == 0 else n_cols
    c_lo = n_cols // c_hi
    gx = Gather(x_all, x_ref, r_hi, r_lo, r, lambda h, l: (h * r_lo + l, c), xh_send, xh_recv, xl_send, xl_recv)
    gy = Gather(y_all, y_ref, c_hi, c_lo, c, lambda h, l: (r, h * c_lo + l), yh_send, yh_recv, yl_send, yl_recv)
    gx.step(0)
    gy.step(0)
    x_all[pl.ds(pl.multiple_of(r * block, block), block), :] = x_ref[...]
    y_all[pl.ds(pl.multiple_of(c * block, block), block), :] = y_ref[...]

    squares = y_ref[...].astype(jnp.float32) ** 2
    high = squares.astype(jnp.bfloat16)
    low = (squares - high.astype(jnp.float32)).astype(jnp.bfloat16)
    ones = jnp.ones((16, width), jnp.bfloat16)
    dims = (((1,), (1,)), ((), ()))
    sq = lax.dot_general(ones, high, dims, preferred_element_type=jnp.float32)
    sq = sq + lax.dot_general(ones, low, dims, preferred_element_type=jnp.float32)
    y_aux[c, 0:8, :] = sq[0:8] * (-0.5 * unit)
    y_aux[c, 8:16, :] = jnp.broadcast_to(jnp.log2(smass_ref[pl.ds(r, 1), :]), (8, block))
    x_aux[r, :, :] = jnp.broadcast_to(jnp.log2(lmass_ref[pl.ds(c, 1), :]), (8, block))
    for d in range(1, n_rows):
        push(x_aux.at[r], x_aux.at[r], xa_send.at[d], xa_recv.at[d], (lax.rem(r + d, n_rows), c))
    for d in range(1, n_cols):
        push(y_aux.at[c], y_aux.at[c], ya_send.at[d], ya_recv.at[d], (r, lax.rem(c + d, n_cols)))

    for j in range(1, r_hi):
        gx.step(j)
    for j in range(r_hi):
        for e in range(1, r_lo):
            gx.cross(j, e)

    def fill(cb):
        ys = y_all[pl.ds(pl.multiple_of(cb * block, block), block), :]

        @pl.loop(0, lots // 256)
        def _(i):
            rows = pl.ds(pl.multiple_of(i * 256, 256), 256)
            inner = lax.dot_general(x_all[rows, :], ys, dims, preferred_element_type=jnp.float32) * unit
            for t in range(per):
                tile[cb * per + t, rows, :] = inner[:, t * LANES : (t + 1) * LANES]

    fill(c)
    for j in range(1, c_hi):
        cb = gy.step(j)
        fill(cb)
        for e in range(1, c_lo):
            fill(gy.cross(j - 1, e))
    for e in range(1, c_lo):
        fill(gy.cross(c_hi - 1, e))

    for d in range(1, n_rows):
        landed(x_aux.at[lax.rem(r + n_rows - d, n_rows)], xa_send.at[d], xa_recv.at[d])
    for d in range(1, n_cols):
        landed(y_aux.at[lax.rem(c + n_cols - d, n_cols)], ya_send.at[d], ya_recv.at[d])
    for n in range(slot_groups):
        cut = slice((n % per) * LANES, (n % per + 1) * LANES)
        g_dense[n : n + 1, :] = y_aux[n // per, 0:1, cut]
        mg[n : n + 1, :] = y_aux[n // per, 8:9, cut]
    for n in range(lot_groups):
        cut = slice((n % per) * LANES, (n % per + 1) * LANES)
        mf[n : n + 1, :] = x_aux[n // per, 0:1, cut]

    for it in range(ITERS):
        @pl.loop(0, lot_groups)
        def _(b):
            pots = [g_dense[n : n + 1, :] for n in range(slot_groups)]
            pieces = []
            for q in range(LANES // 16):
                rows = pl.ds(pl.multiple_of(b * LANES + q * 16, 16), 16)
                pieces.append(lse_rows([tile[n, rows, :] + pots[n] for n in range(slot_groups)]))
            turned = jnp.concatenate(pieces, axis=0).T
            top = jnp.max(turned, axis=0, keepdims=True)
            total = jnp.sum(jnp.exp2(turned - top), axis=0, keepdims=True)
            row_parts[it, r, pl.ds(b, 1), :] = top + jnp.log2(total)

        for d in range(1, n_rows):
            here = row_parts.at[it, r]
            push(here, here, row_send.at[it, d], row_recv.at[it, d], (lax.rem(r + d, n_rows), c))
        for d in range(1, n_rows):
            landed(row_parts.at[it, lax.rem(r + n_rows - d, n_rows)], row_send.at[it, d], row_recv.at[it, d])
        f_dense = mf[...] - lse_rows([row_parts[it, k] for k in range(n_rows)])
        for n in range(lot_groups):
            f_col[n * LANES : (n + 1) * LANES, :] = jnp.broadcast_to(f_dense[n : n + 1, :], (LANES, LANES)).T

        @pl.loop(0, slot_groups)
        def _(n):
            tops, totals = [], []
            for q in range(lots // LANES):
                rows = slice(q * LANES, (q + 1) * LANES)
                score = (tile[n, rows, :] + f_col[rows, :]).reshape(LANES // 8, 8, LANES)
                top = jnp.max(score, axis=0)
                tops.append(top)
                totals.append(jnp.sum(jnp.exp2(score - top[None]), axis=0))
            top = jnp.max(functools.reduce(jnp.maximum, tops), axis=0, keepdims=True)
            total = functools.reduce(jnp.add, [s * jnp.exp2(t - top) for s, t in zip(totals, tops)])
            total = jnp.sum(total, axis=0, keepdims=True)
            col_parts[it, c, pl.ds(n, 1), :] = top + jnp.log2(total)

        for d in range(1, n_cols):
            here = col_parts.at[it, c]
            push(here, here, col_send.at[it, d], col_recv.at[it, d], (r, lax.rem(c + d, n_cols)))
        for d in range(1, n_cols):
            landed(col_parts.at[it, lax.rem(c + n_cols - d, n_cols)], col_send.at[it, d], col_recv.at[it, d])
        g_dense[...] = mg[...] - lse_rows([col_parts[it, k] for k in range(n_cols)])

    chunk = 64

    def share(lb):
        base = pl.multiple_of(lb * block, block)

        @pl.loop(0, block // chunk)
        def _(i):
            rows = pl.ds(pl.multiple_of(base + i * chunk, chunk), chunk)
            here = pl.ds(pl.multiple_of(i * chunk, chunk), chunk)
            pots = f_col[rows, :]
            total = jnp.zeros((chunk, LANES), jnp.float32)
            for n in range(slot_groups):
                part = jnp.exp2(tile[n, rows, :] + g_dense[n : n + 1, :] + pots)
                total = total + part
                plan[here, n * LANES : (n + 1) * LANES] = part.astype(jnp.bfloat16)
            row_sum[here, :] = jnp.broadcast_to(jnp.sum(total, axis=1, keepdims=True), (chunk, LANES))

        moved = jnp.dot(plan[...], y_all[...], preferred_element_type=jnp.float32)
        return row_sum[:, 0:1] * x_all[pl.ds(base, block), :].astype(jnp.float32) - moved

    h, core = r // r_lo, lax.rem(r, r_lo)
    for d in list(range(1, r_hi)) + [0]:
        to_h = lax.rem(h + d, r_hi)
        for e in range(1, r_lo):
            to_l = lax.rem(core + e, r_lo)
            sib_out[d, e] = share(to_h * r_lo + to_l).astype(jnp.bfloat16)
            push(sib_out.at[d, e], sib_in.at[d, e], sib_send.at[d, e], sib_recv.at[d, e], (h * r_lo + to_l, c))
        acc[...] = share(to_h * r_lo + core)
        for e in range(1, r_lo):
            landed(sib_in.at[d, e], sib_send.at[d, e], sib_recv.at[d, e])
            acc[...] += sib_in[d, e].astype(jnp.float32)
        if d:
            far_out[d] = acc[...].astype(jnp.bfloat16)
            push(far_out.at[d], far_in.at[d], far_send.at[d], far_recv.at[d], (to_h * r_lo + core, c))
    for d in range(1, r_hi):
        landed(far_in.at[d], far_send.at[d], far_recv.at[d])
        acc[...] += far_in[d].astype(jnp.float32)
    out_ref[...] = acc[...]

    for copy, when in pending:
        if when is None:
            copy.wait_send()
        else:
            pl.when(when)(copy.wait_send)


def local(n_rows, n_cols, lot_features, slot_features, lot_mass, slot_mass):
    block, width = lot_features.shape
    lots, slots = n_rows * block, n_cols * block
    f32, bf16 = jnp.float32, jnp.bfloat16
    r_lo = 2 if n_rows % 2 == 0 else 1
    r_hi = n_rows // r_lo
    c_hi = 4 if n_cols % 4 == 0 else n_cols
    c_lo = n_cols // c_hi
    dma = pltpu.SemaphoreType.DMA
    sems = [
        dma((2, r_hi)), dma((r_hi,)), dma((r_lo, r_hi)), dma((r_lo, r_hi)),
        dma((2, c_hi)), dma((c_hi,)), dma((c_lo, c_hi)), dma((c_lo, c_hi)),
        dma((n_rows,)), dma((n_rows,)), dma((n_cols,)), dma((n_cols,)),
        dma((ITERS, n_rows)), dma((ITERS, n_rows)), dma((ITERS, n_cols)), dma((ITERS, n_cols)),
        dma((r_hi, r_lo)), dma((r_hi, r_lo)), dma((r_hi,)), dma((r_hi,)),
    ]
    vmem = pltpu.VMEM
    return pl.pallas_call(
        functools.partial(kernel, n_rows, n_cols),
        out_shape=jax.ShapeDtypeStruct((block, width), f32),
        in_specs=[pl.BlockSpec(memory_space=vmem)] * 4,
        out_specs=pl.BlockSpec(memory_space=vmem),
        scratch_shapes=[
            vmem((lots, width), bf16),
            vmem((slots, width), bf16),
            vmem((slots // LANES, lots, LANES), f32),
            vmem((n_rows, 8, block), f32),
            vmem((n_cols, 16, block), f32),
            vmem((lots, LANES), f32),
            vmem((slots // LANES, LANES), f32),
            vmem((lots // LANES, LANES), f32),
            vmem((slots // LANES, LANES), f32),
            vmem((ITERS, n_rows, lots // LANES, LANES), f32),
            vmem((ITERS, n_cols, slots // LANES, LANES), f32),
            vmem((block, slots), bf16),
            vmem((block, LANES), f32),
            vmem((r_hi, r_lo, block, width), bf16),
            vmem((r_hi, r_lo, block, width), bf16),
            vmem((r_hi, block, width), bf16),
            vmem((r_hi, block, width), bf16),
            vmem((block, width), f32),
        ] + sems,
        compiler_params=pltpu.CompilerParams(
            collective_id=0, has_side_effects=True, vmem_limit_bytes=48 * 1024 * 1024
        ),
        cost_estimate=pl.CostEstimate(
            flops=4 * lots * slots * width,
            bytes_accessed=4 * block * width * 2,
            transcendentals=7 * lots * slots,
        ),
    )(
        lot_features, slot_features,
        lot_mass.reshape(n_cols, block), slot_mass.reshape(n_rows, block),
    )


def solution(mesh):
    placed = (P(("rows", "cols"), None), P(("cols", "rows"), None), P("rows"), P("cols"))
    return jax.shard_map(
        functools.partial(local, mesh.shape["rows"], mesh.shape["cols"]),
        mesh=mesh, in_specs=placed, out_specs=P(("rows", "cols"), None), check_vma=False,
    )
```

time: 521 us -> 89.1 us (0.17)
  blocking collectives: 234 us -> 0 us
  waiting for transfers between devices: 200 us -> 0 us
  Pallas kernels: 0 us -> 85.5 us
  other arithmetic: 54 us -> 0 us
  between operations: 13.5 us -> 0.02 us
  matrix products: 12.3 us -> 0 us
    all_gather x12 -> x0, blocking collectives: 214 us -> none  [combined_all(): pieces = jax.tree.map(lambda part: lax.all_gather(part, axis), value)]
    psum x1 -> x0, waiting for transfers between devices: 128 us -> none  [local(): moved_sum, row_sum = lax.psum((moved, row_total), 'cols')]
    pallas_call x0 -> x1, Pallas kernels: none -> 85.5 us  [local(): pl.pallas_call(functools.partial(kernel, n_rows, n_cols), out_shape=jax.S...]
    all_gather x2 -> x0, waiting for transfers between devices: 70.3 us -> none  [the longest x1 49.9 us: local(): lot_full = lax.all_gather(lot_features, 'cols', axis=0, tiled=True)]
    reduce_sum x9 -> x0, other arithmetic: 28.7 us -> none  [the longest x3 10.7 us: local(): totals = jnp.sum(jnp.exp(scores - peaks[None, :]), axis=0)]
    reduce_max x5 -> x0, other arithmetic: 20.2 us -> none  [the longest x3 12.2 us: local(): peaks = jnp.max(scores, axis=0)]
    psum x1 -> x0, blocking collectives: 20 us -> none  [local(): moved_sum, row_sum = lax.psum((moved, row_total), 'cols')]
    dot_general x2 -> x0, matrix products: 12.3 us -> none  [the longest x1 7.89 us: local(): jnp.dot(plan.astype(jnp.bfloat16), slot_full, preferred_element_type=jnp....]
  transfers between devices with their start and end apart: 3 -> 0, of which waited for: 3 -> 0; matrix products, arithmetic and copies ran while one was open for 2% -> 0% of each run, Pallas kernels for 0% -> 0%
where the time goes in v1:
time: 89.1 us; the launch traced here: 88.9 us
  Pallas kernels  85.5 us (96%)
  local copies, waits for them, and re-layouts  3.4 us (4%)
    pallas_call x1, Pallas kernels, local(): pl.pallas_call(functools.partial(kernel, n_rows, n_cols), out_shape=jax.S...  85.5 us
    unnamed x7, local copies, waits for them, and re-layouts  2.69 us

profile of v1, /device:TPU:0, one launch (start us, length us, event | category | flops | bytes accessed | tf_op | source)
XLA Modules:
  0.0 88.9 jit_solution(9375191868382766442)
XLA Ops:
  0.0 0.0 copy-start.2
  0.0 0.7 reshape.7.smass_ref
  0.7 0.0 copy-done.2
  0.7 0.0 copy-start
  0.7 0.9 %copy-done = bf16[256,512]{1,0:T(8,128)(2,1)S(1)} copy-done((bf16[256,512]{1,0:T(8,128)(2,1)S(1)}, bf16[256,512]{1,0:T(8,128)(2,1)}, u32[]{:S(2)}) %copy-start) | copy-done | bytes 262168
  1.7 0.0 copy-start.1
  1.7 0.9 %copy-done.1 = bf16[256,512]{1,0:T(8,128)(2,1)S(1)} copy-done((bf16[256,512]{1,0:T(8,128)(2,1)S(1)}, bf16[256,512]{1,0:T(8,128)(2,1)}, u32[]{:S(2)}) %copy-start.1) | copy-done | bytes 262168
  2.6 85.5 %shard_map.46 = f32[256,512]{1,0:T(8,128)S(1)} custom-call(bf16[256,512]{1,0:T(8,128)(2,1)S(1)} %copy-done, bf16[256,512]{1,0:T(8,128)(2,1)S(1)} %copy-done.1, f32[8,256]{1,0:T(8,128)S(1)} %reshape.6.lmass_ref, f32[4,256]{1,0:T(4,128)S(1)} %reshape.7.smass_ref), custom_call_target="tpu_custom_call" | custom-call | flops 4294967296 | bytes 1048576 | tf_op jit(solution)/shard_map/pallas_call | solution.py:289
  88.1 0.8 copy.6
  (1 shorter events, 0.0 us)
Async XLA Ops:
  0.0 0.7 copy-start.2
  0.7 1.0 %copy-start = (bf16[256,512]{1,0:T(8,128)(2,1)S(1)}, bf16[256,512]{1,0:T(8,128)(2,1)}, u32[]{:S(2)}) copy-start(bf16[256,512]{1,0:T(8,128)(2,1)} %x_ref.1) | copy-start | bytes 786436
  1.7 0.9 %copy-start.1 = (bf16[256,512]{1,0:T(8,128)(2,1)S(1)}, bf16[256,512]{1,0:T(8,128)(2,1)}, u32[]{:S(2)}) copy-start(bf16[256,512]{1,0:T(8,128)(2,1)} %y_ref.1) | copy-start | bytes 786436

commit v2 on v1

--- a/solution.py
+++ b/solution.py
@@ -41,7 +41,7 @@
     row_parts, col_parts, plan, row_sum, sib_out, sib_in, far_out, far_in, acc,
     xh_send, xh_recv, xl_send, xl_recv, yh_send, yh_recv, yl_send, yl_recv,
     xa_send, xa_recv, ya_send, ya_recv, row_send, row_recv, col_send, col_recv,
-    sib_send, sib_recv, far_send, far_recv,
+    sib_send, sib_recv, far_send, far_recv, own_sem, peak, total_ref, col_peak, col_total,
 ):
     r = lax.axis_index("rows")
     c = lax.axis_index("cols")
@@ -125,10 +125,17 @@
     gy = Gather(y_all, y_ref, c_hi, c_lo, c, lambda h, l: (r, h * c_lo + l), yh_send, yh_recv, yl_send, yl_recv)
     gx.step(0)
     gy.step(0)
-    x_all[pl.ds(pl.multiple_of(r * block, block), block), :] = x_ref[...]
-    y_all[pl.ds(pl.multiple_of(c * block, block), block), :] = y_ref[...]
-
-    squares = y_ref[...].astype(jnp.float32) ** 2
+    own_y = pl.ds(pl.multiple_of(c * block, block), block)
+    own_x = pl.ds(pl.multiple_of(r * block, block), block)
+    mine = [
+        pltpu.make_async_copy(y_ref, y_all.at[own_y, :], own_sem.at[0]),
+        pltpu.make_async_copy(x_ref, x_all.at[own_x, :], own_sem.at[1]),
+    ]
+    for copy in mine:
+        copy.start()
+    mine[0].wait()
+
+    squares = y_all[own_y, :].astype(jnp.float32) ** 2
     high = squares.astype(jnp.bfloat16)
     low = (squares - high.astype(jnp.float32)).astype(jnp.bfloat16)
     ones = jnp.ones((16, width), jnp.bfloat16)
@@ -143,23 +150,37 @@
     for d in range(1, n_cols):
         push(y_aux.at[c], y_aux.at[c], ya_send.at[d], ya_recv.at[d], (r, lax.rem(c + d, n_cols)))
 
+    mine[1].wait()
     for j in range(1, r_hi):
         gx.step(j)
     for j in range(r_hi):
         for e in range(1, r_lo):
             gx.cross(j, e)
 
-    def fill(cb):
+    def fill(cb, first=False):
         ys = y_all[pl.ds(pl.multiple_of(cb * block, block), block), :]
 
         @pl.loop(0, lots // 256)
         def _(i):
             rows = pl.ds(pl.multiple_of(i * 256, 256), 256)
             inner = lax.dot_general(x_all[rows, :], ys, dims, preferred_element_type=jnp.float32) * unit
+            parts = [inner[:, t * LANES : (t + 1) * LANES] for t in range(per)]
             for t in range(per):
-                tile[cb * per + t, rows, :] = inner[:, t * LANES : (t + 1) * LANES]
-
-    fill(c)
+                tile[cb * per + t, rows, :] = parts[t]
+            scores = [parts[t] + y_aux[cb, 0:1, t * LANES : (t + 1) * LANES] for t in range(per)]
+            top = functools.reduce(jnp.maximum, scores)
+            if not first:
+                before = peak[rows, :]
+                top = jnp.maximum(top, before)
+            sums = functools.reduce(jnp.add, [jnp.exp2(score - top) for score in scores])
+            if not first:
+                sums = sums + total_ref[rows, :] * jnp.exp2(before - top)
+            peak[rows, :] = top
+            total_ref[rows, :] = sums
+
+    fill(c, True)
+    for d in range(1, n_cols):
+        landed(y_aux.at[lax.rem(c + n_cols - d, n_cols)], ya_send.at[d], ya_recv.at[d])
     for j in range(1, c_hi):
         cb = gy.step(j)
         fill(cb)
@@ -170,28 +191,28 @@
 
     for d in range(1, n_rows):
         landed(x_aux.at[lax.rem(r + n_rows - d, n_rows)], xa_send.at[d], xa_recv.at[d])
-    for d in range(1, n_cols):
-        landed(y_aux.at[lax.rem(c + n_cols - d, n_cols)], ya_send.at[d], ya_recv.at[d])
     for n in range(slot_groups):
         cut = slice((n % per) * LANES, (n % per + 1) * LANES)
-        g_dense[n : n + 1, :] = y_aux[n // per, 0:1, cut]
         mg[n : n + 1, :] = y_aux[n // per, 8:9, cut]
     for n in range(lot_groups):
         cut = slice((n % per) * LANES, (n % per + 1) * LANES)
         mf[n : n + 1, :] = x_aux[n // per, 0:1, cut]
 
     for it in range(ITERS):
-        @pl.loop(0, lot_groups)
-        def _(b):
-            pots = [g_dense[n : n + 1, :] for n in range(slot_groups)]
-            pieces = []
-            for q in range(LANES // 16):
-                rows = pl.ds(pl.multiple_of(b * LANES + q * 16, 16), 16)
-                pieces.append(lse_rows([tile[n, rows, :] + pots[n] for n in range(slot_groups)]))
-            turned = jnp.concatenate(pieces, axis=0).T
+        if it:
+            @pl.loop(0, lot_groups)
+            def _(b):
+                pots = [g_dense[n : n + 1, :] for n in range(slot_groups)]
+                for q in range(LANES // 16):
+                    rows = pl.ds(pl.multiple_of(b * LANES + q * 16, 16), 16)
+                    peak[rows, :] = lse_rows([tile[n, rows, :] + pots[n] for n in range(slot_groups)])
+
+        for b in range(lot_groups):
+            rows = slice(b * LANES, (b + 1) * LANES)
+            turned = (peak[rows, :] if it else peak[rows, :] + jnp.log2(total_ref[rows, :])).T
             top = jnp.max(turned, axis=0, keepdims=True)
             total = jnp.sum(jnp.exp2(turned - top), axis=0, keepdims=True)
-            row_parts[it, r, pl.ds(b, 1), :] = top + jnp.log2(total)
+            row_parts[it, r, b : b + 1, :] = top + jnp.log2(total)
 
         for d in range(1, n_rows):
             here = row_parts.at[it, r]
@@ -211,10 +232,14 @@
                 top = jnp.max(score, axis=0)
                 tops.append(top)
                 totals.append(jnp.sum(jnp.exp2(score - top[None]), axis=0))
-            top = jnp.max(functools.reduce(jnp.maximum, tops), axis=0, keepdims=True)
-            total = functools.reduce(jnp.add, [s * jnp.exp2(t - top) for s, t in zip(totals, tops)])
-            total = jnp.sum(total, axis=0, keepdims=True)
-            col_parts[it, c, pl.ds(n, 1), :] = top + jnp.log2(total)
+            top = functools.reduce(jnp.maximum, tops)
+            col_peak[n] = top
+            col_total[n] = functools.reduce(jnp.add, [s * jnp.exp2(t - top) for s, t in zip(totals, tops)])
+
+        for n in range(slot_groups):
+            top = jnp.max(col_peak[n], axis=0, keepdims=True)
+            total = jnp.sum(col_total[n] * jnp.exp2(col_peak[n] - top), axis=0, keepdims=True)
+            col_parts[it, c, n : n + 1, :] = top + jnp.log2(total)
 
         for d in range(1, n_cols):
             here = col_parts.at[it, c]
@@ -289,7 +314,7 @@
     return pl.pallas_call(
         functools.partial(kernel, n_rows, n_cols),
         out_shape=jax.ShapeDtypeStruct((block, width), f32),
-        in_specs=[pl.BlockSpec(memory_space=vmem)] * 4,
+        in_specs=[pl.BlockSpec(memory_space=pl.ANY)] * 2 + [pl.BlockSpec(memory_space=vmem)] * 2,
         out_specs=pl.BlockSpec(memory_space=vmem),
         scratch_shapes=[
             vmem((lots, width), bf16),
@@ -310,7 +335,13 @@
             vmem((r_hi, block, width), bf16),
             vmem((r_hi, block, width), bf16),
             vmem((block, width), f32),
-        ] + sems,
+        ] + sems + [
+            dma((2,)),
+            vmem((lots, LANES), f32),
+            vmem((lots, LANES), f32),
+            vmem((slots // LANES, 8, LANES), f32),
+            vmem((slots // LANES, 8, LANES), f32),
+        ],
         compiler_params=pltpu.CompilerParams(
             collective_id=0, has_side_effects=True, vmem_limit_bytes=48 * 1024 * 1024
         ),

time: 89.1 us -> 86.8 us (0.974)
  Pallas kernels: 85.5 us -> 83.1 us
    pallas_call x1, Pallas kernels: 85.5 us -> 83.1 us  [local(): pl.pallas_call(functools.partial(kernel, n_rows, n_cols), out_shape=jax.S...]
where the time goes in v2:
time: 86.8 us; the launch traced here: 86.6 us
  Pallas kernels  83.1 us (96%)
  local copies, waits for them, and re-layouts  3.4 us (4%)
    pallas_call x1, Pallas kernels, local(): pl.pallas_call(functools.partial(kernel, n_rows, n_cols), out_shape=jax.S...  83.1 us
    unnamed x7, local copies, waits for them, and re-layouts  2.69 us

profile of v2, /device:TPU:0, one launch (start us, length us, event | category | flops | bytes accessed | tf_op | source)
XLA Modules:
  0.0 86.6 jit_solution(5700901378559262281)
XLA Ops:
  0.0 0.0 copy-start.2
  0.0 0.7 reshape.7.smass_ref
  0.7 0.0 copy-done.2
  0.7 0.0 copy-start
  0.7 0.9 %copy-done = bf16[256,512]{1,0:T(8,128)(2,1)S(1)} copy-done((bf16[256,512]{1,0:T(8,128)(2,1)S(1)}, bf16[256,512]{1,0:T(8,128)(2,1)}, u32[]{:S(2)}) %copy-start) | copy-done | bytes 262168
  1.7 0.0 copy-start.1
  1.7 0.9 %copy-done.1 = bf16[256,512]{1,0:T(8,128)(2,1)S(1)} copy-done((bf16[256,512]{1,0:T(8,128)(2,1)S(1)}, bf16[256,512]{1,0:T(8,128)(2,1)}, u32[]{:S(2)}) %copy-start.1) | copy-done | bytes 262168
  2.6 83.1 %shard_map.46 = f32[256,512]{1,0:T(8,128)S(1)} custom-call(bf16[256,512]{1,0:T(8,128)(2,1)S(1)} %copy-done, bf16[256,512]{1,0:T(8,128)(2,1)S(1)} %copy-done.1, f32[8,256]{1,0:T(8,128)S(1)} %reshape.6.lmass_ref, f32[4,256]{1,0:T(4,128)S(1)} %reshape.7.smass_ref), custom_call_target="tpu_custom_call" | custom-call | flops 4294967296 | bytes 1048576 | tf_op jit(solution)/shard_map/pallas_call | solution.py:314
  85.8 0.8 copy.6
  (1 shorter events, 0.0 us)
Async XLA Ops:
  0.0 0.7 copy-start.2
  0.7 1.0 %copy-start = (bf16[256,512]{1,0:T(8,128)(2,1)S(1)}, bf16[256,512]{1,0:T(8,128)(2,1)}, u32[]{:S(2)}) copy-start(bf16[256,512]{1,0:T(8,128)(2,1)} %x_ref.1) | copy-start | bytes 786436
  1.7 0.9 %copy-start.1 = (bf16[256,512]{1,0:T(8,128)(2,1)S(1)}, bf16[256,512]{1,0:T(8,128)(2,1)}, u32[]{:S(2)}) copy-start(bf16[256,512]{1,0:T(8,128)(2,1)} %y_ref.1) | copy-start | bytes 786436

commit v3 on v2

--- a/solution.py
+++ b/solution.py
@@ -9,6 +9,7 @@
 from jax.sharding import PartitionSpec as P
 
 ITERS = 3
+PIECES = 2
 LANES = 128
 LOG2E = 1.0 / math.log(2.0)
 MESH = pl.DeviceIdType.MESH
@@ -41,7 +42,7 @@
     row_parts, col_parts, plan, row_sum, sib_out, sib_in, far_out, far_in, acc,
     xh_send, xh_recv, xl_send, xl_recv, yh_send, yh_recv, yl_send, yl_recv,
     xa_send, xa_recv, ya_send, ya_recv, row_send, row_recv, col_send, col_recv,
-    sib_send, sib_recv, far_send, far_recv, own_sem, peak, total_ref, col_peak, col_total,
+    sib_send, sib_recv, far_send, far_recv, own_sem, peak, total_ref, col_peak, col_total, mass,
 ):
     r = lax.axis_index("rows")
     c = lax.axis_index("cols")
@@ -86,36 +87,42 @@
             self.sems = h_send, h_recv, l_send, l_recv
             self.table = near_first(hi)
 
-        def place(self, h, l):
-            return pl.ds(pl.multiple_of((h * self.lo + l) * block, block), block)
-
-        def step(self, j):
+        def place(self, h, l, p):
+            rows = block // PIECES
+            return pl.ds(pl.multiple_of((h * self.lo + l) * block + p * rows, rows), rows)
+
+        def source(self, j):
+            return self.h if j == 0 else pick(self.table, self.h, j)
+
+        def number(self, j, e=0):
+            return self.source(j) * self.lo + lax.rem(self.l + e, self.lo)
+
+        def step(self, j, p):
             h_send, h_recv, l_send, l_recv = self.sems
-            src_h = self.h if j == 0 else pick(self.table, self.h, j)
-            dst = self.buf.at[self.place(src_h, self.l)]
+            src_h = self.source(j)
+            dst = self.buf.at[self.place(src_h, self.l, p)]
             if j == 0:
-                src = self.own
+                src = self.own.at[pl.ds(p * (block // PIECES), block // PIECES)]
                 for way in (0, 1):
                     to = self.h + (2 * way - 1)
                     ok = jnp.logical_and(to >= 0, to < self.hi)
-                    push(src, dst, h_send.at[way, 0], h_recv.at[src_h], self.target(to, self.l), ok)
+                    push(src, dst, h_send.at[way, 0, p], h_recv.at[src_h, p], self.target(to, self.l), ok)
             else:
                 src = dst
-                landed(dst, h_send.at[0, j], h_recv.at[src_h])
+                landed(dst, h_send.at[0, j, p], h_recv.at[src_h, p])
                 to = jnp.where(src_h < self.h, self.h + 1, self.h - 1)
                 ok = jnp.logical_and(to >= 0, to < self.hi)
-                push(src, dst, h_send.at[0, j], h_recv.at[src_h], self.target(to, self.l), ok)
+                push(src, dst, h_send.at[0, j, p], h_recv.at[src_h, p], self.target(to, self.l), ok)
             for e in range(1, self.lo):
                 to = lax.rem(self.l + e, self.lo)
-                push(src, dst, l_send.at[e, j], l_recv.at[self.l, src_h], self.target(self.h, to))
-            return src_h * self.lo + self.l
+                push(src, dst, l_send.at[e, j, p], l_recv.at[self.l, src_h, p], self.target(self.h, to))
 
         def cross(self, j, e):
             _, _, l_send, l_recv = self.sems
-            src_h = self.h if j == 0 else pick(self.table, self.h, j)
+            src_h = self.source(j)
             src_l = lax.rem(self.l + e, self.lo)
-            landed(self.buf.at[self.place(src_h, src_l)], l_send.at[e, j], l_recv.at[src_l, src_h])
-            return src_h * self.lo + src_l
+            for p in range(PIECES):
+                landed(self.buf.at[self.place(src_h, src_l, p)], l_send.at[e, j, p], l_recv.at[src_l, src_h, p])
 
     r_lo = 2 if n_rows % 2 == 0 else 1
     r_hi = n_rows // r_lo
@@ -123,8 +130,9 @@
     c_lo = n_cols // c_hi
     gx = Gather(x_all, x_ref, r_hi, r_lo, r, lambda h, l: (h * r_lo + l, c), xh_send, xh_recv, xl_send, xl_recv)
     gy = Gather(y_all, y_ref, c_hi, c_lo, c, lambda h, l: (r, h * c_lo + l), yh_send, yh_recv, yl_send, yl_recv)
-    gx.step(0)
-    gy.step(0)
+    for p in range(PIECES):
+        gy.step(0, p)
+        gx.step(0, p)
     own_y = pl.ds(pl.multiple_of(c * block, block), block)
     own_x = pl.ds(pl.multiple_of(r * block, block), block)
     mine = [
@@ -133,6 +141,14 @@
     ]
     for copy in mine:
         copy.start()
+    masses = [
+        pltpu.make_async_copy(lmass_ref.at[own_y], mass.at[0], own_sem.at[2]),
+        pltpu.make_async_copy(smass_ref.at[own_x], mass.at[1], own_sem.at[3]),
+    ]
+    for copy in masses:
+        copy.start()
+    for copy in masses:
+        copy.wait()
     mine[0].wait()
 
     squares = y_all[own_y, :].astype(jnp.float32) ** 2
@@ -143,16 +159,23 @@
     sq = lax.dot_general(ones, high, dims, preferred_element_type=jnp.float32)
     sq = sq + lax.dot_general(ones, low, dims, preferred_element_type=jnp.float32)
     y_aux[c, 0:8, :] = sq[0:8] * (-0.5 * unit)
-    y_aux[c, 8:16, :] = jnp.broadcast_to(jnp.log2(smass_ref[pl.ds(r, 1), :]), (8, block))
-    x_aux[r, :, :] = jnp.broadcast_to(jnp.log2(lmass_ref[pl.ds(c, 1), :]), (8, block))
+    y_aux[c, 8:16, :] = jnp.broadcast_to(jnp.log2(mass[1:2, :]), (8, block))
+    x_aux[r, :, :] = jnp.broadcast_to(jnp.log2(mass[0:1, :]), (8, block))
     for d in range(1, n_rows):
         push(x_aux.at[r], x_aux.at[r], xa_send.at[d], xa_recv.at[d], (lax.rem(r + d, n_rows), c))
     for d in range(1, n_cols):
         push(y_aux.at[c], y_aux.at[c], ya_send.at[d], ya_recv.at[d], (r, lax.rem(c + d, n_cols)))
 
     mine[1].wait()
+    early = min(3, c_hi)
+    gy.step(1, 0)
     for j in range(1, r_hi):
-        gx.step(j)
+        for p in range(PIECES):
+            gx.step(j, p)
+    for p in range(PIECES):
+        for j in range(1, early):
+            if p or j > 1:
+                gy.step(j, p)
     for j in range(r_hi):
         for e in range(1, r_lo):
             gx.cross(j, e)
@@ -181,13 +204,24 @@
     fill(c, True)
     for d in range(1, n_cols):
         landed(y_aux.at[lax.rem(c + n_cols - d, n_cols)], ya_send.at[d], ya_recv.at[d])
-    for j in range(1, c_hi):
-        cb = gy.step(j)
-        fill(cb)
+    def fill_crossed(j):
         for e in range(1, c_lo):
-            fill(gy.cross(j - 1, e))
-    for e in range(1, c_lo):
-        fill(gy.cross(c_hi - 1, e))
+            gy.cross(j, e)
+            fill(gy.number(j, e))
+
+    fill_crossed(0)
+    late = [(j, p) for j in range(early, c_hi) for p in range(PIECES)]
+    for j in range(1, early):
+        if late:
+            gy.step(*late.pop(0))
+        fill(gy.number(j))
+    for j, p in late:
+        gy.step(j, p)
+    fill_crossed(1)
+    for j in range(early, c_hi):
+        fill(gy.number(j))
+    for j in range(2, c_hi):
+        fill_crossed(j)
 
     for d in range(1, n_rows):
         landed(x_aux.at[lax.rem(r + n_rows - d, n_rows)], xa_send.at[d], xa_recv.at[d])
@@ -250,10 +284,10 @@
 
     chunk = 64
 
-    def share(lb):
-        base = pl.multiple_of(lb * block, block)
-
-        @pl.loop(0, block // chunk)
+    def share(lb, start, count):
+        base = pl.multiple_of(lb * block + start, count)
+
+        @pl.loop(0, count // chunk)
         def _(i):
             rows = pl.ds(pl.multiple_of(base + i * chunk, chunk), chunk)
             here = pl.ds(pl.multiple_of(i * chunk, chunk), chunk)
@@ -265,26 +299,40 @@
                 plan[here, n * LANES : (n + 1) * LANES] = part.astype(jnp.bfloat16)
             row_sum[here, :] = jnp.broadcast_to(jnp.sum(total, axis=1, keepdims=True), (chunk, LANES))
 
-        moved = jnp.dot(plan[...], y_all[...], preferred_element_type=jnp.float32)
-        return row_sum[:, 0:1] * x_all[pl.ds(base, block), :].astype(jnp.float32) - moved
+        moved = jnp.dot(plan[0:count, :], y_all[...], preferred_element_type=jnp.float32)
+        return row_sum[0:count, 0:1] * x_all[pl.ds(base, count), :].astype(jnp.float32) - moved
 
     h, core = r // r_lo, lax.rem(r, r_lo)
+    half = block // PIECES
     for d in list(range(1, r_hi)) + [0]:
         to_h = lax.rem(h + d, r_hi)
-        for e in range(1, r_lo):
-            to_l = lax.rem(core + e, r_lo)
-            sib_out[d, e] = share(to_h * r_lo + to_l).astype(jnp.bfloat16)
-            push(sib_out.at[d, e], sib_in.at[d, e], sib_send.at[d, e], sib_recv.at[d, e], (h * r_lo + to_l, c))
-        acc[...] = share(to_h * r_lo + core)
-        for e in range(1, r_lo):
-            landed(sib_in.at[d, e], sib_send.at[d, e], sib_recv.at[d, e])
-            acc[...] += sib_in[d, e].astype(jnp.float32)
-        if d:
-            far_out[d] = acc[...].astype(jnp.bfloat16)
-            push(far_out.at[d], far_in.at[d], far_send.at[d], far_recv.at[d], (to_h * r_lo + core, c))
+        cuts = [(p, p * half, half) for p in range(PIECES)] if d else [(0, 0, block)]
+        for p, start, count in cuts:
+            cut = slice(start, start + count)
+            for e in range(1, r_lo):
+                to_l = lax.rem(core + e, r_lo)
+                sib_out[d, e, cut, :] = share(to_h * r_lo + to_l, start, count).astype(jnp.bfloat16)
+                push(
+                    sib_out.at[d, e, cut], sib_in.at[d, e, cut], sib_send.at[d, e, p], sib_recv.at[d, e, p],
+                    (h * r_lo + to_l, c),
+                )
+            part = share(to_h * r_lo + core, start, count)
+            for e in range(1, r_lo):
+                landed(sib_in.at[d, e, cut], sib_send.at[d, e, p], sib_recv.at[d, e, p])
+                part = part + sib_in[d, e, cut, :].astype(jnp.float32)
+            if d:
+                far_out[d, cut, :] = part.astype(jnp.bfloat16)
+                push(
+                    far_out.at[d, cut], far_in.at[d, cut], far_send.at[d, p], far_recv.at[d, p],
+                    (to_h * r_lo + core, c),
+                )
+            else:
+                acc[...] = part
     for d in range(1, r_hi):
-        landed(far_in.at[d], far_send.at[d], far_recv.at[d])
-        acc[...] += far_in[d].astype(jnp.float32)
+        for p in range(PIECES):
+            cut = slice(p * half, (p + 1) * half)
+            landed(far_in.at[d, cut], far_send.at[d, p], far_recv.at[d, p])
+            acc[cut, :] += far_in[d, cut, :].astype(jnp.float32)
     out_ref[...] = acc[...]
 
     for copy, when in pending:
@@ -304,17 +352,17 @@
     c_lo = n_cols // c_hi
     dma = pltpu.SemaphoreType.DMA
     sems = [
-        dma((2, r_hi)), dma((r_hi,)), dma((r_lo, r_hi)), dma((r_lo, r_hi)),
-        dma((2, c_hi)), dma((c_hi,)), dma((c_lo, c_hi)), dma((c_lo, c_hi)),
+        dma((2, r_hi, PIECES)), dma((r_hi, PIECES)), dma((r_lo, r_hi, PIECES)), dma((r_lo, r_hi, PIECES)),
+        dma((2, c_hi, PIECES)), dma((c_hi, PIECES)), dma((c_lo, c_hi, PIECES)), dma((c_lo, c_hi, PIECES)),
         dma((n_rows,)), dma((n_rows,)), dma((n_cols,)), dma((n_cols,)),
         dma((ITERS, n_rows)), dma((ITERS, n_rows)), dma((ITERS, n_cols)), dma((ITERS, n_cols)),
-        dma((r_hi, r_lo)), dma((r_hi, r_lo)), dma((r_hi,)), dma((r_hi,)),
+        dma((r_hi, r_lo, PIECES)), dma((r_hi, r_lo, PIECES)), dma((r_hi, PIECES)), dma((r_hi, PIECES)),
     ]
     vmem = pltpu.VMEM
     return pl.pallas_call(
         functools.partial(kernel, n_rows, n_cols),
         out_shape=jax.ShapeDtypeStruct((block, width), f32),
-        in_specs=[pl.BlockSpec(memory_space=pl.ANY)] * 2 + [pl.BlockSpec(memory_space=vmem)] * 2,
+        in_specs=[pl.BlockSpec(memory_space=pl.ANY)] * 4,
         out_specs=pl.BlockSpec(memory_space=vmem),
         scratch_shapes=[
             vmem((lots, width), bf16),
@@ -336,14 +384,15 @@
             vmem((r_hi, block, width), bf16),
             vmem((block, width), f32),
         ] + sems + [
-            dma((2,)),
+            dma((4,)),
             vmem((lots, LANES), f32),
             vmem((lots, LANES), f32),
             vmem((slots // LANES, 8, LANES), f32),
             vmem((slots // LANES, 8, LANES), f32),
+            vmem((2, block), f32),
         ],
         compiler_params=pltpu.CompilerParams(
-            collective_id=0, has_side_effects=True, vmem_limit_bytes=48 * 1024 * 1024
+            collective_id=0, has_side_effects=True, vmem_limit_bytes=62 * 1024 * 1024
         ),
         cost_estimate=pl.CostEstimate(
             flops=4 * lots * slots * width,
@@ -352,7 +401,7 @@
         ),
     )(
         lot_features, slot_features,
-        lot_mass.reshape(n_cols, block), slot_mass.reshape(n_rows, block),
+        lot_mass, slot_mass,
     )
 
 

time: 86.8 us -> 79.4 us (0.915)
  Pallas kernels: 83.1 us -> 77.3 us
  local copies, waits for them, and re-layouts: 3.4 us -> 1.87 us
    pallas_call x1, Pallas kernels: 83.1 us -> 77.3 us  [local(): pl.pallas_call(functools.partial(kernel, n_rows, n_cols), out_shape=jax.S...]
    unnamed x7 -> x1, local copies, waits for them, and re-layouts: 2.69 us -> 1.87 us
where the time goes in v3:
time: 79.4 us; the launch traced here: 79.2 us
  Pallas kernels  77.3 us (97%)
  local copies, waits for them, and re-layouts  1.87 us (2%)
    pallas_call x1, Pallas kernels, local(): pl.pallas_call(functools.partial(kernel, n_rows, n_cols), out_shape=jax.S...  77.3 us
    unnamed x1, local copies, waits for them, and re-layouts  1.87 us

profile of v3, /device:TPU:0, one launch (start us, length us, event | category | flops | bytes accessed | tf_op | source)
XLA Modules:
  0.0 79.2 jit_solution(2220887131911391083)
XLA Ops:
  0.0 77.3 %shard_map.46 = f32[256,512]{1,0:T(8,128)} custom-call(bf16[256,512]{1,0:T(8,128)(2,1)} %x_ref.1, bf16[256,512]{1,0:T(8,128)(2,1)} %y_ref.1, f32[2048]{0:T(1024)} %lmass_ref.1, f32[1024]{0:T(1024)} %smass_ref.1), custom_call_target="tpu_custom_call" | custom-call | flops 4294967296 | bytes 1048576 | tf_op jit(solution)/shard_map/pallas_call | solution.py:362
  77.3 1.9 %copy.6 = f32[256,512]{1,0:T(8,128)} copy(f32[256,512]{1,0:T(8,128)} %shard_map.46) | data formatting | bytes 1048576

commit v4 on v3

--- a/solution.py
+++ b/solution.py
@@ -232,55 +232,124 @@
         cut = slice((n % per) * LANES, (n % per + 1) * LANES)
         mf[n : n + 1, :] = x_aux[n // per, 0:1, cut]
 
+    lot_half, slot_half = lot_groups // 2, slot_groups // 2
+
+    def send_rows(it, half):
+        for d in range(1, n_rows):
+            here = row_parts.at[it, half, r]
+            push(here, here, row_send.at[it, half, d], row_recv.at[it, half, d], (lax.rem(r + d, n_rows), c))
+
+    def take_rows(it, half):
+        for d in range(1, n_rows):
+            there = row_parts.at[it, half, lax.rem(r + n_rows - d, n_rows)]
+            landed(there, row_send.at[it, half, d], row_recv.at[it, half, d])
+        first = half * lot_half
+        logs = mf[first : first + lot_half, :]
+        f_dense = logs - lse_rows([row_parts[it, half, k] for k in range(n_rows)])
+        for n in range(lot_half):
+            rows = slice((first + n) * LANES, (first + n + 1) * LANES)
+            f_col[rows, :] = jnp.broadcast_to(f_dense[n : n + 1, :], (LANES, LANES)).T
+
+    def send_cols(it, half):
+        for d in range(1, n_cols):
+            here = col_parts.at[it, half, c]
+            push(here, here, col_send.at[it, half, d], col_recv.at[it, half, d], (r, lax.rem(c + d, n_cols)))
+
+    def take_cols(it, half):
+        for d in range(1, n_cols):
+            there = col_parts.at[it, half, lax.rem(c + n_cols - d, n_cols)]
+            landed(there, col_send.at[it, half, d], col_recv.at[it, half, d])
+        groups = slice(half * slot_half, (half + 1) * slot_half)
+        g_dense[groups, :] = mg[groups, :] - lse_rows([col_parts[it, half, k] for k in range(n_cols)])
+
+    def row_scores(half, rows, pots):
+        return [tile[half * slot_half + n, rows, :] + pots[n] for n in range(slot_half)]
+
+    def row_pots(half):
+        return [g_dense[half * slot_half + n : half * slot_half + n + 1, :] for n in range(slot_half)]
+
+    def row_first():
+        @pl.loop(0, lot_groups)
+        def _(b):
+            pots = row_pots(0)
+            for q in range(LANES // 16):
+                rows = pl.ds(pl.multiple_of(b * LANES + q * 16, 16), 16)
+                scores = row_scores(0, rows, pots)
+                top = functools.reduce(jnp.maximum, scores)
+                peak[rows, :] = top
+                total_ref[rows, :] = functools.reduce(jnp.add, [jnp.exp2(score - top) for score in scores])
+
+    def row_second(half):
+        @pl.loop(half * lot_half, (half + 1) * lot_half)
+        def _(b):
+            pots = row_pots(1)
+            for q in range(LANES // 16):
+                rows = pl.ds(pl.multiple_of(b * LANES + q * 16, 16), 16)
+                scores = row_scores(1, rows, pots)
+                before = peak[rows, :]
+                top = jnp.maximum(functools.reduce(jnp.maximum, scores), before)
+                sums = functools.reduce(jnp.add, [jnp.exp2(score - top) for score in scores])
+                peak[rows, :] = top
+                total_ref[rows, :] = sums + total_ref[rows, :] * jnp.exp2(before - top)
+
+    def row_close(it, half):
+        for b in range(lot_half):
+            rows = slice((half * lot_half + b) * LANES, (half * lot_half + b + 1) * LANES)
+            turned = (peak[rows, :] + jnp.log2(total_ref[rows, :])).T
+            top = jnp.max(turned, axis=0, keepdims=True)
+            total = jnp.sum(jnp.exp2(turned - top), axis=0, keepdims=True)
+            row_parts[it, half, r, b : b + 1, :] = top + jnp.log2(total)
+
+    def col_scan(n, half):
+        tops, totals = [], []
+        span = lots // 2
+        for q in range(span // LANES):
+            rows = slice(half * span + q * LANES, half * span + (q + 1) * LANES)
+            score = (tile[n, rows, :] + f_col[rows, :]).reshape(LANES // 8, 8, LANES)
+            top = jnp.max(score, axis=0)
+            tops.append(top)
+            totals.append(jnp.sum(jnp.exp2(score - top[None]), axis=0))
+        if half:
+            tops.append(col_peak[n])
+            totals.append(col_total[n])
+        top = functools.reduce(jnp.maximum, tops)
+        col_peak[n] = top
+        col_total[n] = functools.reduce(jnp.add, [s * jnp.exp2(t - top) for s, t in zip(totals, tops)])
+
+    def col_close(it, half):
+        for n in range(slot_half):
+            top8 = col_peak[half * slot_half + n]
+            top = jnp.max(top8, axis=0, keepdims=True)
+            total = jnp.sum(col_total[half * slot_half + n] * jnp.exp2(top8 - top), axis=0, keepdims=True)
+            col_parts[it, half, c, n : n + 1, :] = top + jnp.log2(total)
+
     for it in range(ITERS):
         if it:
-            @pl.loop(0, lot_groups)
-            def _(b):
-                pots = [g_dense[n : n + 1, :] for n in range(slot_groups)]
-                for q in range(LANES // 16):
-                    rows = pl.ds(pl.multiple_of(b * LANES + q * 16, 16), 16)
-                    peak[rows, :] = lse_rows([tile[n, rows, :] + pots[n] for n in range(slot_groups)])
-
-        for b in range(lot_groups):
-            rows = slice(b * LANES, (b + 1) * LANES)
-            turned = (peak[rows, :] if it else peak[rows, :] + jnp.log2(total_ref[rows, :])).T
-            top = jnp.max(turned, axis=0, keepdims=True)
-            total = jnp.sum(jnp.exp2(turned - top), axis=0, keepdims=True)
-            row_parts[it, r, b : b + 1, :] = top + jnp.log2(total)
-
-        for d in range(1, n_rows):
-            here = row_parts.at[it, r]
-            push(here, here, row_send.at[it, d], row_recv.at[it, d], (lax.rem(r + d, n_rows), c))
-        for d in range(1, n_rows):
-            landed(row_parts.at[it, lax.rem(r + n_rows - d, n_rows)], row_send.at[it, d], row_recv.at[it, d])
-        f_dense = mf[...] - lse_rows([row_parts[it, k] for k in range(n_rows)])
-        for n in range(lot_groups):
-            f_col[n * LANES : (n + 1) * LANES, :] = jnp.broadcast_to(f_dense[n : n + 1, :], (LANES, LANES)).T
-
-        @pl.loop(0, slot_groups)
+            take_cols(it - 1, 0)
+            row_first()
+            take_cols(it - 1, 1)
+        for half in (0, 1):
+            if it:
+                row_second(half)
+            row_close(it, half)
+            send_rows(it, half)
+
+        take_rows(it, 0)
+
+        @pl.loop(0, slot_groups, unroll=4)
         def _(n):
-            tops, totals = [], []
-            for q in range(lots // LANES):
-                rows = slice(q * LANES, (q + 1) * LANES)
-                score = (tile[n, rows, :] + f_col[rows, :]).reshape(LANES // 8, 8, LANES)
-                top = jnp.max(score, axis=0)
-                tops.append(top)
-                totals.append(jnp.sum(jnp.exp2(score - top[None]), axis=0))
-            top = functools.reduce(jnp.maximum, tops)
-            col_peak[n] = top
-            col_total[n] = functools.reduce(jnp.add, [s * jnp.exp2(t - top) for s, t in zip(totals, tops)])
-
-        for n in range(slot_groups):
-            top = jnp.max(col_peak[n], axis=0, keepdims=True)
-            total = jnp.sum(col_total[n] * jnp.exp2(col_peak[n] - top), axis=0, keepdims=True)
-            col_parts[it, c, n : n + 1, :] = top + jnp.log2(total)
-
-        for d in range(1, n_cols):
-            here = col_parts.at[it, c]
-            push(here, here, col_send.at[it, d], col_recv.at[it, d], (r, lax.rem(c + d, n_cols)))
-        for d in range(1, n_cols):
-            landed(col_parts.at[it, lax.rem(c + n_cols - d, n_cols)], col_send.at[it, d], col_recv.at[it, d])
-        g_dense[...] = mg[...] - lse_rows([col_parts[it, k] for k in range(n_cols)])
+            col_scan(n, 0)
+
+        take_rows(it, 1)
+        for half in (0, 1):
+            @pl.loop(half * slot_half, (half + 1) * slot_half, unroll=4)
+            def _(n):
+                col_scan(n, 1)
+
+            col_close(it, half)
+            send_cols(it, half)
+    for half in (0, 1):
+        take_cols(ITERS - 1, half)
 
     chunk = 64
 
@@ -355,14 +424,14 @@
         dma((2, r_hi, PIECES)), dma((r_hi, PIECES)), dma((r_lo, r_hi, PIECES)), dma((r_lo, r_hi, PIECES)),
         dma((2, c_hi, PIECES)), dma((c_hi, PIECES)), dma((c_lo, c_hi, PIECES)), dma((c_lo, c_hi, PIECES)),
         dma((n_rows,)), dma((n_rows,)), dma((n_cols,)), dma((n_cols,)),
-        dma((ITERS, n_rows)), dma((ITERS, n_rows)), dma((ITERS, n_cols)), dma((ITERS, n_cols)),
+        dma((ITERS, 2, n_rows)), dma((ITERS, 2, n_rows)), dma((ITERS, 2, n_cols)), dma((ITERS, 2, n_cols)),
         dma((r_hi, r_lo, PIECES)), dma((r_hi, r_lo, PIECES)), dma((r_hi, PIECES)), dma((r_hi, PIECES)),
     ]
     vmem = pltpu.VMEM
     return pl.pallas_call(
         functools.partial(kernel, n_rows, n_cols),
         out_shape=jax.ShapeDtypeStruct((block, width), f32),
-        in_specs=[pl.BlockSpec(memory_space=pl.ANY)] * 4,
+        in_specs=[pl.BlockSpec(memory_space=pltpu.HBM)] * 4,
         out_specs=pl.BlockSpec(memory_space=vmem),
         scratch_shapes=[
             vmem((lots, width), bf16),
@@ -374,8 +443,8 @@
             vmem((slots // LANES, LANES), f32),
             vmem((lots // LANES, LANES), f32),
             vmem((slots // LANES, LANES), f32),
-            vmem((ITERS, n_rows, lots // LANES, LANES), f32),
-            vmem((ITERS, n_cols, slots // LANES, LANES), f32),
+            vmem((ITERS, 2, n_rows, lots // LANES // 2, LANES), f32),
+            vmem((ITERS, 2, n_cols, slots // LANES // 2, LANES), f32),
             vmem((block, slots), bf16),
             vmem((block, LANES), f32),
             vmem((r_hi, r_lo, block, width), bf16),

time: 79.4 us -> 77.6 us (0.977)
  Pallas kernels: 77.3 us -> 75.6 us
    pallas_call x1, Pallas kernels: 77.3 us -> 75.6 us  [local(): pl.pallas_call(functools.partial(kernel, n_rows, n_cols), out_shape=jax.S...]
where the time goes in v4:
time: 77.6 us; the launch traced here: 77.5 us
  Pallas kernels  75.6 us (97%)
  local copies, waits for them, and re-layouts  1.87 us (2%)
    pallas_call x1, Pallas kernels, local(): pl.pallas_call(functools.partial(kernel, n_rows, n_cols), out_shape=jax.S...  75.6 us
    unnamed x1, local copies, waits for them, and re-layouts  1.87 us

profile of v4, /device:TPU:0, one launch (start us, length us, event | category | flops | bytes accessed | tf_op | source)
XLA Modules:
  0.0 77.5 jit_solution(17072041573100610390)
XLA Ops:
  0.0 75.6 %shard_map.46 = f32[256,512]{1,0:T(8,128)} custom-call(bf16[256,512]{1,0:T(8,128)(2,1)} %x_ref.1, bf16[256,512]{1,0:T(8,128)(2,1)} %y_ref.1, f32[2048]{0:T(1024)} %lmass_ref.1, f32[1024]{0:T(1024)} %smass_ref.1), custom_call_target="tpu_custom_call" | custom-call | flops 4294967296 | bytes 1048576 | tf_op jit(solution)/shard_map/pallas_call | solution.py:431
  75.6 1.9 %copy.6 = f32[256,512]{1,0:T(8,128)} copy(f32[256,512]{1,0:T(8,128)} %shard_map.46) | data formatting | bytes 1048576

commit v5 on v4

--- a/solution.py
+++ b/solution.py
@@ -269,7 +269,7 @@
         return [g_dense[half * slot_half + n : half * slot_half + n + 1, :] for n in range(slot_half)]
 
     def row_first():
-        @pl.loop(0, lot_groups)
+        @pl.loop(0, lot_groups, unroll=2)
         def _(b):
             pots = row_pots(0)
             for q in range(LANES // 16):
@@ -280,7 +280,7 @@
                 total_ref[rows, :] = functools.reduce(jnp.add, [jnp.exp2(score - top) for score in scores])
 
     def row_second(half):
-        @pl.loop(half * lot_half, (half + 1) * lot_half)
+        @pl.loop(half * lot_half, (half + 1) * lot_half, unroll=2)
         def _(b):
             pots = row_pots(1)
             for q in range(LANES // 16):
@@ -353,23 +353,22 @@
 
     chunk = 64
 
-    def share(lb, start, count):
+    def share(lb, start, count, turn):
         base = pl.multiple_of(lb * block + start, count)
 
-        @pl.loop(0, count // chunk)
-        def _(i):
+        for i in range(count // chunk):
             rows = pl.ds(pl.multiple_of(base + i * chunk, chunk), chunk)
-            here = pl.ds(pl.multiple_of(i * chunk, chunk), chunk)
+            here = slice(i * chunk, (i + 1) * chunk)
             pots = f_col[rows, :]
             total = jnp.zeros((chunk, LANES), jnp.float32)
             for n in range(slot_groups):
                 part = jnp.exp2(tile[n, rows, :] + g_dense[n : n + 1, :] + pots)
                 total = total + part
-                plan[here, n * LANES : (n + 1) * LANES] = part.astype(jnp.bfloat16)
-            row_sum[here, :] = jnp.broadcast_to(jnp.sum(total, axis=1, keepdims=True), (chunk, LANES))
-
-        moved = jnp.dot(plan[0:count, :], y_all[...], preferred_element_type=jnp.float32)
-        return row_sum[0:count, 0:1] * x_all[pl.ds(base, count), :].astype(jnp.float32) - moved
+                plan[turn, here, n * LANES : (n + 1) * LANES] = part.astype(jnp.bfloat16)
+            row_sum[turn, here, :] = jnp.broadcast_to(jnp.sum(total, axis=1, keepdims=True), (chunk, LANES))
+
+        moved = jnp.dot(plan[turn, 0:count, :], y_all[...], preferred_element_type=jnp.float32)
+        return row_sum[turn, 0:count, 0:1] * x_all[pl.ds(base, count), :].astype(jnp.float32) - moved
 
     h, core = r // r_lo, lax.rem(r, r_lo)
     half = block // PIECES
@@ -380,12 +379,12 @@
             cut = slice(start, start + count)
             for e in range(1, r_lo):
                 to_l = lax.rem(core + e, r_lo)
-                sib_out[d, e, cut, :] = share(to_h * r_lo + to_l, start, count).astype(jnp.bfloat16)
+                sib_out[d, e, cut, :] = share(to_h * r_lo + to_l, start, count, 0).astype(jnp.bfloat16)
                 push(
                     sib_out.at[d, e, cut], sib_in.at[d, e, cut], sib_send.at[d, e, p], sib_recv.at[d, e, p],
                     (h * r_lo + to_l, c),
                 )
-            part = share(to_h * r_lo + core, start, count)
+            part = share(to_h * r_lo + core, start, count, 1)
             for e in range(1, r_lo):
                 landed(sib_in.at[d, e, cut], sib_send.at[d, e, p], sib_recv.at[d, e, p])
                 part = part + sib_in[d, e, cut, :].astype(jnp.float32)
@@ -397,12 +396,13 @@
                 )
             else:
                 acc[...] = part
-    for d in range(1, r_hi):
-        for p in range(PIECES):
-            cut = slice(p * half, (p + 1) * half)
+    for p in range(PIECES):
+        cut = slice(p * half, (p + 1) * half)
+        result = acc[cut, :]
+        for d in range(1, r_hi):
             landed(far_in.at[d, cut], far_send.at[d, p], far_recv.at[d, p])
-            acc[cut, :] += far_in[d, cut, :].astype(jnp.float32)
-    out_ref[...] = acc[...]
+            result = result + far_in[d, cut, :].astype(jnp.float32)
+        out_ref[cut, :] = result
 
     for copy, when in pending:
         if when is None:
@@ -445,8 +445,8 @@
             vmem((slots // LANES, LANES), f32),
             vmem((ITERS, 2, n_rows, lots // LANES // 2, LANES), f32),
             vmem((ITERS, 2, n_cols, slots // LANES // 2, LANES), f32),
-            vmem((block, slots), bf16),
-            vmem((block, LANES), f32),
+            vmem((2, block, slots), bf16),
+            vmem((2, block, LANES), f32),
             vmem((r_hi, r_lo, block, width), bf16),
             vmem((r_hi, r_lo, block, width), bf16),
             vmem((r_hi, block, width), bf16),

time: 77.6 us -> 77.1 us (level)
  no operation moved by 1% of the time
where the time goes in v5:
time: 77.1 us; the launch traced here: 76.9 us
  Pallas kernels  75 us (97%)
  local copies, waits for them, and re-layouts  1.87 us (2%)
    pallas_call x1, Pallas kernels, local(): pl.pallas_call(functools.partial(kernel, n_rows, n_cols), out_shape=jax.S...  75 us
    unnamed x1, local copies, waits for them, and re-layouts  1.87 us

profile of v5, /device:TPU:0, one launch (start us, length us, event | category | flops | bytes accessed | tf_op | source)
XLA Modules:
  0.0 76.9 jit_solution(5419420986786336977)
XLA Ops:
  0.0 75.0 %shard_map.46 = f32[256,512]{1,0:T(8,128)} custom-call(bf16[256,512]{1,0:T(8,128)(2,1)} %x_ref.1, bf16[256,512]{1,0:T(8,128)(2,1)} %y_ref.1, f32[2048]{0:T(1024)} %lmass_ref.1, f32[1024]{0:T(1024)} %smass_ref.1), custom_call_target="tpu_custom_call" | custom-call | flops 4294967296 | bytes 1048576 | tf_op jit(solution)/shard_map/pallas_call | solution.py:431
  75.1 1.9 %copy.6 = f32[256,512]{1,0:T(8,128)} copy(f32[256,512]{1,0:T(8,128)} %shard_map.46) | data formatting | bytes 1048576
